TPU v7x, 32 devices: a whole 2x2x4 slice. The times are simulated.
32 devices in a mesh: dp: 2 (over x), hid: 4 (over y, core), mod: 4 (over z).
Axes of the slice: x: 2, y: 2, z: 4, core: 2. Of those that a mesh axis runs over, the one named last changes fastest.
Arguments:
- tokens: bfloat16 [16928, 768], P(('dp', 'hid', 'mod')), may hold values from -6 to 6
- cotangent: bfloat16 [16928, 768], P(('dp', 'hid', 'mod')), may hold values from -6 to 6
- unit_kind: int32 [32], replicated, may hold values from 0 to 1, as said below
- unit_len: int32 [32, 2], replicated, may hold values from 1 to 529, as said below
- pack_offset: int32 [32], replicated, may hold values from 1 to 529, as said below
- norm1_gain: float32 [768], replicated, may hold values from 0.5 to 1.5
- norm1_bias: float32 [768], replicated, may hold values from -1.8 to 1.8
- qkv_weight: bfloat16 [3, 768, 768], P(None, 'hid'), may hold values from -0.21875 to 0.21875
- out_weight: bfloat16 [768, 768], P('hid'), may hold values from -3 to 3
- norm2_gain: float32 [768], replicated, may hold values from 0.5 to 1.5
- norm2_bias: float32 [768], replicated, may hold values from -1.8 to 1.8
- up_weight: bfloat16 [768, 3072], P('mod', 'hid'), may hold values from -0.21875 to 0.21875
- down_weight: bfloat16 [768, 3072], P('mod', 'hid'), may hold values from -0.109375 to 0.109375
Outputs:
- output: bfloat16 [16928, 768], P(('dp', 'hid', 'mod'))
- tokens_grad: bfloat16 [16928, 768], P(('dp', 'hid', 'mod'))
- norm1_gain_grad: float32 [768], replicated
- norm1_bias_grad: float32 [768], replicated
- qkv_weight_grad: float32 [3, 768, 768], P(None, 'hid')
- out_weight_grad: float32 [768, 768], P('hid')
- norm2_gain_grad: float32 [768], replicated
- norm2_bias_grad: float32 [768], replicated
- up_weight_grad: float32 [768, 3072], P('mod', 'hid')
- down_weight_grad: float32 [768, 3072], P('mod', 'hid')
Inputs may be any that keep to these rules, and one draw needn't show every extreme that they name: `unit_kind`: kind 0 is one strip of unit_len[n, 0] patches; kind 1 packs two half strips. `unit_len`: for kind 1 both lengths are at most 264; column 1 is used only for kind 1. For kind 1, unit_len[n, 0] <= pack_offset[n] <= 529 - unit_len[n, 1]; unused for kind 0.
All inputs are finite; a program needn't handle non-finite values.
Results may differ from a plain program's by a relative error of at most 0.012.
The roundings to bfloat16 on the way count: a program that leaves them out, or rounds other values in their place, can miss the bound.
Values may be sent and summed in bfloat16 or wider, within the bound.
No kernel may reach another device: no remote copies, remote signals or barrier semaphores. Data moves between devices by JAX's collectives and lax.ppermute only.
A program may use at most 192 MiB of HBM per device.

v0:
```python
import jax
import jax.numpy as jnp
from jax import lax
from jax.sharding import PartitionSpec as P

HEAD = 64
U = 529


EPSILON = 1e-06
MASKED = -1000000000.0


def exact_gelu(values):
    return jax.nn.gelu(values, approximate=False)


def norm_forward(stream, gain, bias):
    row_mean = jnp.mean(stream, axis=1, keepdims=True)
    spread = jnp.mean(stream * stream, axis=1, keepdims=True) - row_mean * row_mean
    inverse = lax.rsqrt(spread + EPSILON)
    centred = (stream - row_mean) * inverse
    return (centred * gain + bias, centred, inverse)


def norm_backward(upstream, centred, inverse, gain):
    scaled = upstream * gain
    first_mean = jnp.mean(scaled, axis=1, keepdims=True)
    second_mean = jnp.mean(scaled * centred, axis=1, keepdims=True)
    result = inverse * (scaled - first_mean - centred * second_mean)
    return (result, jnp.sum(upstream * centred, axis=0), jnp.sum(upstream, axis=0))


def matmul_rows(source, weight, transposed):
    if transposed:
        return lax.dot_general(
            source, weight, (((1,), (1,)), ((), ())), preferred_element_type=jnp.float32
        )
    return jnp.dot(source, weight, preferred_element_type=jnp.float32)


def gather_wide(local_rows):
    return lax.all_gather(local_rows, "hid", axis=0, tiled=True)


def heads_total(partial_term, row_count):
    return lax.psum_scatter(
        partial_term(jnp.int32(0), lax.axis_size("hid") * row_count),
        "hid",
        scatter_dimension=0,
        tiled=True,
    )


def grid_enter(local_rows):
    grid_local = lax.all_to_all(local_rows, "mod", split_axis=1, concat_axis=0, tiled=True)
    return (grid_local, lax.all_gather(grid_local, "hid", axis=0, tiled=True))


def sum_over_model(source, weight):
    row_count = source.shape[0] // lax.axis_size("mod")

    def partial_term(begin_row, count):
        return matmul_rows(source, weight, False)

    return lax.psum_scatter(
        partial_term(jnp.int32(0), lax.axis_size("mod") * row_count),
        "mod",
        scatter_dimension=0,
        tiled=True,
    )


def gather_columns(local_rows):
    return lax.all_gather(local_rows, "mod", axis=0, tiled=True)


def sum_over_hidden(source, weight):
    row_count = source.shape[0] // lax.axis_size("hid")

    def partial_term(begin_row, count):
        return matmul_rows(source, weight, True)

    grid_result = lax.psum_scatter(
        partial_term(jnp.int32(0), lax.axis_size("hid") * row_count),
        "hid",
        scatter_dimension=0,
        tiled=True,
    )
    return lax.all_to_all(grid_result, "mod", split_axis=0, concat_axis=1, tiled=True)


def column_product(left_rows, right_rows):
    return lax.dot_general(
        left_rows, right_rows, (((0,), (0,)), ((), ())), preferred_element_type=jnp.float32
    )


def unit_mask(kind_one, lengths, offset):
    position = jnp.arange(U, dtype=jnp.int32)
    start_pos = jnp.where(kind_one == 1, offset, U)
    upper_part = position >= start_pos
    key_valid = jnp.where(upper_part, position - start_pos < lengths[1], position < lengths[0])
    return (upper_part[:, None] == upper_part[None, :]) & key_valid[None, :]


def unit_scores(queries, key_heads, allowed):
    scores = jnp.einsum(
        "qhd,khd->hqk", queries, key_heads, preferred_element_type=jnp.float32
    ) * HEAD ** (-0.5)
    return jnp.where(allowed[None], scores, MASKED)


def attend_forward(unit_items):
    queries, key_heads, value_heads, kind_one, lengths, offset = unit_items
    scores = unit_scores(queries, key_heads, unit_mask(kind_one, lengths, offset))
    row_max = jnp.max(scores, axis=-1, keepdims=True)
    exponent = jnp.exp(scores - row_max)
    row_total = jnp.sum(exponent, axis=-1, keepdims=True)
    probabilities = (exponent / row_total).astype(jnp.bfloat16)
    mixed_heads = jnp.einsum(
        "hqk,khd->qhd", probabilities, value_heads, preferred_element_type=jnp.float32
    )
    return (mixed_heads.astype(jnp.bfloat16), (row_max + jnp.log(row_total))[..., 0])


def attend_backward(unit_items):
    queries, key_heads, value_heads, upstream, logsum, kind_one, lengths, offset = unit_items
    scores = unit_scores(queries, key_heads, unit_mask(kind_one, lengths, offset))
    probabilities = jnp.exp(scores - logsum[..., None])
    rounded = probabilities.astype(jnp.bfloat16)
    d_weights = jnp.einsum(
        "qhd,khd->hqk", upstream, value_heads, preferred_element_type=jnp.float32
    )
    d_values = jnp.einsum("hqk,qhd->khd", rounded, upstream, preferred_element_type=jnp.float32)
    d_scores = probabilities * (
        d_weights - jnp.sum(probabilities * d_weights, axis=-1, keepdims=True)
    )
    d_scores = d_scores.astype(jnp.bfloat16)
    factor = HEAD ** (-0.5)
    d_queries = (
        jnp.einsum("hqk,khd->qhd", d_scores, key_heads, preferred_element_type=jnp.float32) * factor
    )
    d_keys = (
        jnp.einsum("hqk,qhd->khd", d_scores, queries, preferred_element_type=jnp.float32) * factor
    )
    return jnp.stack([d_queries, d_keys, d_values], axis=1).astype(jnp.bfloat16)


def body(
    tokens,
    cotangent,
    unit_kind,
    unit_len,
    pack_offset,
    norm1_gain,
    norm1_bias,
    qkv_weight,
    out_weight,
    norm2_gain,
    norm2_bias,
    up_weight,
    down_weight,
):
    local_count = tokens.shape[0]
    units_here = local_count // U
    hid_count = lax.axis_size("hid")
    mod_count = lax.axis_size("mod")
    heads_here = qkv_weight.shape[1] // HEAD
    head_width = qkv_weight.shape[1]
    block_index = jnp.arange(hid_count, dtype=jnp.int32)[:, None]
    inner_index = jnp.arange(units_here, dtype=jnp.int32)[None, :]
    unit_ids = (
        ((lax.axis_index("dp") * hid_count + block_index) * mod_count + lax.axis_index("mod"))
        * units_here
        + inner_index
    ).reshape(-1)
    unit_kinds = jnp.take(unit_kind, unit_ids, axis=0)
    lengths = jnp.take(unit_len, unit_ids, axis=0)
    offsets = jnp.take(pack_offset, unit_ids, axis=0)
    wide_units = hid_count * units_here
    stream = tokens.astype(jnp.float32)
    normed1, centred1, inverse1 = norm_forward(stream, norm1_gain, norm1_bias)
    inputs1 = normed1.astype(jnp.bfloat16)
    inputs1_all = gather_wide(inputs1)
    projected = jnp.einsum(
        "ri,koi->rko", inputs1_all, qkv_weight, preferred_element_type=jnp.float32
    )
    heads_in = projected.astype(jnp.bfloat16).reshape(wide_units, U, 3, heads_here, HEAD)
    queries = heads_in[:, :, 0]
    key_heads = heads_in[:, :, 1]
    value_heads = heads_in[:, :, 2]
    mixed_heads, logsum = lax.map(
        attend_forward, (queries, key_heads, value_heads, unit_kinds, lengths, offsets)
    )
    mixed_flat = mixed_heads.reshape(wide_units * U, head_width)

    def attention_term(begin_row, count):
        return matmul_rows(mixed_flat, out_weight, False)

    attended = heads_total(attention_term, local_count)
    middle = stream + attended
    normed2, centred2, inverse2 = norm_forward(middle, norm2_gain, norm2_bias)
    inputs2 = normed2.astype(jnp.bfloat16)
    inputs2_grid, inputs2_all = grid_enter(inputs2)
    hidden = sum_over_model(inputs2_all, up_weight)
    activated, gelu_pull = jax.vjp(exact_gelu, hidden)
    activated = activated.astype(jnp.bfloat16)
    activated_all = gather_columns(activated)
    branch = sum_over_hidden(activated_all, down_weight)
    output = (middle + branch).astype(jnp.bfloat16)
    upstream_grid, upstream_all = grid_enter(cotangent)
    d_activated = sum_over_model(upstream_all, down_weight)
    d_hidden = gelu_pull(d_activated)[0].astype(jnp.bfloat16)
    down_grad = column_product(upstream_all, activated_all)
    d_hidden_all = gather_columns(d_hidden)
    d_inputs2 = sum_over_hidden(d_hidden_all, up_weight)
    up_grad = column_product(inputs2_all, d_hidden_all)
    up_share, down_share = (
        lax.psum_scatter(
            up_grad.astype(jnp.bfloat16), "dp", scatter_dimension=1, tiled=True
        ).astype(jnp.float32),
        lax.psum_scatter(
            down_grad.astype(jnp.bfloat16), "dp", scatter_dimension=1, tiled=True
        ).astype(jnp.float32),
    )
    up_grad, down_grad = (
        lax.all_gather(up_share.astype(jnp.bfloat16), "dp", axis=1, tiled=True).astype(
            up_share.dtype
        ),
        lax.all_gather(down_share.astype(jnp.bfloat16), "dp", axis=1, tiled=True).astype(
            down_share.dtype
        ),
    )
    d_middle_norm, gain2_grad, bias2_grad = norm_backward(d_inputs2, centred2, inverse2, norm2_gain)
    d_middle = cotangent.astype(jnp.float32) + d_middle_norm
    d_attended = d_middle.astype(jnp.bfloat16)
    d_attended_all = gather_wide(d_attended)
    d_mixed = lax.dot_general(
        d_attended_all, out_weight, (((1,), (1,)), ((), ())), preferred_element_type=jnp.float32
    )
    d_mixed = d_mixed.astype(jnp.bfloat16).reshape(wide_units, U, heads_here, HEAD)
    out_grad = column_product(mixed_flat, d_attended_all)
    d_heads = lax.map(
        attend_backward,
        (queries, key_heads, value_heads, d_mixed, logsum, unit_kinds, lengths, offsets),
    )
    d_heads = d_heads.reshape(wide_units * U, 3, head_width)

    def input_term(begin_row, count):
        return jnp.einsum("rko,koi->ri", d_heads, qkv_weight, preferred_element_type=jnp.float32)

    d_inputs1 = heads_total(input_term, local_count)
    joint_grad = jnp.einsum("rko,ri->koi", d_heads, inputs1_all, preferred_element_type=jnp.float32)
    d_stream_norm, gain1_grad, bias1_grad = norm_backward(d_inputs1, centred1, inverse1, norm1_gain)
    tokens_grad = (d_middle + d_stream_norm).astype(jnp.bfloat16)
    joint_share, out_share = (
        lax.psum_scatter(joint_grad, ("dp", "mod"), scatter_dimension=2, tiled=True),
        lax.psum_scatter(out_grad, ("dp", "mod"), scatter_dimension=1, tiled=True),
    )
    joint_grad, out_grad = (
        lax.all_gather(joint_share.astype(jnp.bfloat16), ("dp", "mod"), axis=2, tiled=True).astype(
            joint_share.dtype
        ),
        lax.all_gather(out_share.astype(jnp.bfloat16), ("dp", "mod"), axis=1, tiled=True).astype(
            out_share.dtype
        ),
    )
    gain1_grad, bias1_grad, gain2_grad, bias2_grad = lax.psum(
        (gain1_grad, bias1_grad, gain2_grad, bias2_grad), ("dp", "hid", "mod")
    )
    return (
        output,
        tokens_grad,
        gain1_grad,
        bias1_grad,
        joint_grad,
        out_grad,
        gain2_grad,
        bias2_grad,
        up_grad,
        down_grad,
    )


def solution(mesh):
    in_specs = (
        P(("dp", "hid", "mod"), None),
        P(("dp", "hid", "mod"), None),
        P(),
        P(),
        P(),
        P(),
        P(),
        P(None, "hid", None),
        P("hid", None),
        P(),
        P(),
        P("mod", "hid"),
        P("mod", "hid"),
    )
    out_specs = (
        P(("dp", "hid", "mod"), None),
        P(("dp", "hid", "mod"), None),
        P(),
        P(),
        P(None, "hid", None),
        P("hid", None),
        P(),
        P(),
        P("mod", "hid"),
        P("mod", "hid"),
    )
    return jax.shard_map(body, mesh=mesh, in_specs=in_specs, out_specs=out_specs, check_vma=False)
```

profile of v0, /device:TPU:0, one launch (start us, length us, event | category | flops | bytes accessed | tf_op | source)
XLA Modules:
  0.0 2332.8 jit_solution(13660564596460135455)
XLA Ops:
  14.4 6.3 all-to-all-start.2
  22.9 22.2 all-to-all-done.2
  65.1 41.4 %while.22 = (s32[]{:T(128)}, bf16[4,529,3,64]{1,3,2,0:T(8,128)(2,1)}, f32[4,3,529]{2,1,0:T(4,128)}, bf16[4,529,3,64]{1,3,2,0:T(8,128)(2,1)}, s32[4]{0:T(128)S(1)...) while((s32[]{:T(128)}, ...), condition=%wide.region_5.7_spmd, body=%wide.region_2.0_spmd.sunk | while | flops 225654464 | bytes 12299442 | solution.py:193
  117.7 60.4 %fusion = f32[536,768]{1,0:T(8,128)} fusion(f32[2116,768]{1,0:T(8,128)} %fusion.95), kind=kCustom, calls=%all-reduce-scatter | all-reduce-scatter fusion | flops 1646593 | bytes 8147456
  198.2 6.2 copy.79
  204.4 6.5 reshape.387
  210.9 14.1 fusion.98
  230.7 436.1 %fusion.2 = f32[2120,768]{1,0:T(8,128)} fusion(f32[8464,768]{1,0:T(8,128)} %fusion.98), kind=kCustom, calls=%all-reduce-scatter.2 | all-reduce-scatter fusion | flops 6512641 | bytes 32514560
  675.9 6.5 reshape.383
  682.4 14.1 fusion.96
  696.6 436.9 %fusion.1 = f32[2120,768]{1,0:T(8,128)} fusion(f32[8464,768]{1,0:T(8,128)} %fusion.96), kind=kCustom, calls=%all-reduce-scatter.1 | all-reduce-scatter fusion | flops 6512641 | bytes 32514560
  1139.7 17.4 concatenate.10
  1157.2 17.4 concatenate.9
  1174.6 16.6 fusion.66
  1191.2 6.8 fusion.67
  1198.8 222.0 %all-gather.21.cloned.1.call-done = bf16[4,2116,768]{2,1,0:T(8,128)(2,1)} async-done(((bf16[1,2116,768]{2,1,0:T(8,128)(2,1)}), bf16[4,2116,768]{2,1,0:T(8,128)(2,1)}) %all-gather.21.cloned.1.call-update) | async-done | bytes 13000720 | tf_op jit(solution)/shard_map/all_gather | solution.py:75
  1420.8 15.0 reshape.389
  1435.8 12.1 fusion.99
  1447.9 198.0 %all-gather.17.cloned.1.call-done = bf16[4,2116,768]{2,1,0:T(8,128)(2,1)} async-done(((bf16[1,2116,768]{2,1,0:T(8,128)(2,1)}), bf16[4,2116,768]{2,1,0:T(8,128)(2,1)}) %all-gather.17.cloned.1.call-update) | async-done | bytes 13000720 | tf_op jit(solution)/shard_map/all_gather | solution.py:75
  1645.9 13.6 reshape.385
  1659.5 11.8 fusion.97
  1672.0 228.3 %all-reduce.14.cloned.1.call-done = (f32[8464,192]{0,1:T(8,128)}, f32[8464,192]{0,1:T(8,128)}) async-done(((f32[8464,192]{0,1:T(8,128)}, f32[8464,192]{0,1:T(8,128)}), (f32[8464,192]{0,1:T(8,128)}, f32[8464,192]{0,1:T(8,128)})) %all-reduce.14.cloned.1.call-update) | async-done | bytes 13000720
  1914.7 8.4 convolution_convert_fusion.3
  1924.5 8.4 fusion.85
  1934.0 25.9 %all-to-all-done.3 = f32[4,529,192]{1,2,0:T(8,128)} async-done(((f32[4,529,192]{1,2,0:T(8,128)}), f32[4,529,192]{1,2,0:T(8,128)}, u32[]{:S(2)}, u32[]{:S(2)}) %all-to-all-start.3) | async-done | bytes 1625120 | tf_op jit(solution)/shard_map/all_to_all | solution.py:90
  2014.7 66.1 %while.23 = (s32[]{:T(128)}, bf16[4,529,3,3,64]{1,4,3,2,0:T(8,128)(2,1)}, bf16[4,529,3,64]{1,3,2,0:T(8,128)(2,1)}, s32[4]{0:T(128)S(1)}, s32[4]{0:T(128)S(1)}, /...) while((s32[]{:T(128)}, ...), condition=%wide.region_17.19_spmd, body=%wide.region_15.18_spmd.sunk | while | flops 552784384 | bytes 34932996 | solution.py:244
  2107.7 7.2 convolution_bitcast_fusion
  2114.9 60.6 %fusion.3 = f32[536,768]{1,0:T(8,128)} fusion(f32[2116,768]{1,0:T(8,128)} %convolution_bitcast_fusion), kind=kCustom, calls=%all-reduce-scatter.3 | all-reduce-scatter fusion | flops 1646593 | bytes 8147456
  2184.6 6.3 concatenate.11
  2208.3 41.1 %all-reduce.10 = (f32[768]{0:T(1024)}, f32[768]{0:T(1024)}, f32[768]{0:T(1024)}, f32[768]{0:T(1024)}) all-reduce(f32[768]{0:T(1024)S(1)} %get-tuple-element.183, f32[768]{0:T(1024)S(1)} %get-tuple-element.236, f32[768]{0:T(1024)S(1)} %get-tuple-element.181, ...), channel_id=1, replica_groups=mesh['dp'=2,'hid'=4,'mod'=4] {'dp','hid','mod'}, use_global_device_ids=true, to_apply=%region_22.24 | all-reduce | flops 3072 | bytes 24576 | tf_op jit(solution)/shard_map/psum | solution.py:269
  2250.5 32.9 %all_gather.37 = bf16[192,768]{0,1:T(8,128)(2,1)S(1)} all-gather(bf16[192,96]{0,1:T(8,128)(2,1)S(1)} %copy.88), channel_id=1, replica_groups=mesh['dp'=2,'hid'=4,'mod'=4] {'dp','mod'}, dimensions={1}, use_global_device_ids=true | all-gather | bytes 331776 | tf_op jit(solution)/shard_map/all_gather | solution.py:265
  2285.8 38.1 %all_gather.36 = bf16[3,192,768]{1,0,2:T(4,128)(2,1)S(1)} all-gather(bf16[3,192,96]{1,0,2:T(4,128)(2,1)S(1)} %copy.87), channel_id=1, replica_groups=mesh['dp'=2,'hid'=4,'mod'=4] {'dp','mod'}, dimensions={2}, use_global_device_ids=true | all-gather | bytes 995328 | tf_op jit(solution)/shard_map/all_gather | solution.py:262
  (292 shorter events, 308.2 us)
Async XLA Ops:
  7.2 44.8 %copy-start = (bf16[3,192,768]{2,1,0:T(8,128)(2,1)S(1)}, bf16[3,192,768]{2,1,0:T(8,128)(2,1)}, u32[]{:S(2)}) copy-start(bf16[3,192,768]{2,1,0:T(8,128)(2,1)} %param.26) | copy-start | bytes 2654212
  7.2 40.2 %all-gather.13.cloned.1.call-start = ((), (), s32[]{:S(2)}) async-start(), calls=%async_computation.8 | async-start | bytes 4116480 | tf_op jit(solution)/shard_map/all_gather | solution.py:43
  9.8 11.0 copy-start.1
  9.8 11.6 copy-start.2
  10.9 11.1 copy-start.22
  14.4 30.6 %all-to-all-start.2 = ((bf16[529,4,192]{0,2,1:T(8,128)(2,1)}), bf16[529,4,192]{0,2,1:T(8,128)(2,1)S(1)}, u32[]{:S(2)}, u32[]{:S(2)}) async-start(bf16[529,4,192]{0,2,1:T(8,128)(2,1)} %bitcast.33), calls=%async_computation.2 | async-start | bytes 1966080 | tf_op jit(solution)/shard_map/all_to_all | solution.py:56
  20.7 177.5 %all-gather.19.cloned.1.call-start = ((), (), s32[]{:S(2)}) async-start(), calls=%async_computation.11 | async-start | bytes 4177920 | tf_op jit(solution)/shard_map/all_gather | solution.py:57
  65.1 47.7 %copy-start.12 = (bf16[192,768]{1,0:T(8,128)(2,1)S(1)}, bf16[192,768]{1,0:T(8,128)(2,1)}, u32[]{:S(2)}) copy-start(bf16[192,768]{1,0:T(8,128)(2,1)} %param.27) | copy-start | bytes 884740
  106.5 11.2 copy-start.5
  106.5 11.2 copy-start.6
  106.5 11.2 copy-start.23
  106.5 11.2 copy-start.25
  117.7 62.6 %copy-start.21 = (u32[32]{0:T(128)S(1)}, u32[32]{0:T(128)}, u32[]{:S(2)}) copy-start(u32[32]{0:T(128)} %constant.177) | copy-start | bytes 388
  179.0 2.6 collective-permute-start
  193.4 31.7 %all-to-all-start = ((bf16[529,4,192]{0,2,1:T(8,128)(2,1)}), bf16[529,4,192]{0,2,1:T(8,128)(2,1)}, u32[]{:S(2)}, u32[]{:S(2)}) async-start(bf16[529,4,192]{0,2,1:T(8,128)(2,1)} %bitcast.233), calls=%async_computation | async-start | bytes 1966080 | tf_op jit(solution)/shard_map/all_to_all | solution.py:56
  197.6 472.1 %all-gather.15.cloned.1.call-start = ((), (), s32[]{:S(2)}) async-start(), calls=%async_computation.9 | async-start | bytes 4177920 | tf_op jit(solution)/shard_map/all_gather | solution.py:57
  230.6 1190.2 %all-gather.21.cloned.1.call-start = ((), (), s32[]{:S(2)}) async-start(), calls=%async_computation.12 | async-start | bytes 16281600 | tf_op jit(solution)/shard_map/all_gather | solution.py:75
  668.2 471.5 %collective-permute-start.2 = (f32[12,768]{1,0:T(8,128)}, f32[12,768]{1,0:T(8,128)S(1)}, u32[]{:S(2)}, u32[]{:S(2)}) collective-permute-start(f32[12,768]{1,0:T(8,128)} %slice.39), channel_id=1, source_target_pairs={{0,1},{1,2},{2,3},{4,5},{5,6},{6,7},{8,9},{9,10},{10,11},{12,13},{... | collective-permute-start | bytes 110600
  1134.9 22.2 collective-permute-start.1
  1174.6 16.6 copy-start.3
  1198.0 447.9 %all-gather.17.cloned.1.call-start = ((), (), s32[]{:S(2)}) async-start(), calls=%async_computation.10 | async-start | bytes 16281600 | tf_op jit(solution)/shard_map/all_gather | solution.py:75
  1198.6 701.7 %all-reduce.14.cloned.1.call-start = ((), (), s32[]{:S(2)}) async-start(), calls=%async_computation.18 | async-start | bytes 26345472
  1910.0 49.9 %all-to-all-start.3 = ((f32[4,529,192]{1,2,0:T(8,128)}), f32[4,529,192]{1,2,0:T(8,128)}, u32[]{:S(2)}, u32[]{:S(2)}) async-start(f32[4,529,192]{1,2,0:T(8,128)} %copy.80), calls=%async_computation.3 | async-start | bytes 3932160 | tf_op jit(solution)/shard_map/all_to_all | solution.py:90
  1914.6 55.1 %reduce-scatter.27.cloned.1.call-start = ((), (), s32[]{:S(2)}) async-start(), calls=%async_computation.16 | async-start | bytes 589824
  1924.1 53.4 %reduce-scatter.29.cloned.1.call-start = ((), (), s32[]{:S(2)}) async-start(), calls=%async_computation.17 | async-start | bytes 589824
  1933.9 64.0 %all-gather.23.cloned.1.call-start = ((), (), s32[]{:S(2)}) async-start(), calls=%async_computation.13 | async-start | bytes 4116480 | tf_op jit(solution)/shard_map/all_gather | solution.py:43
  1988.1 211.0 %all-to-all-start.1 = ((f32[4,529,192]{1,2,0:T(8,128)}), f32[4,529,192]{1,2,0:T(8,128)}, u32[]{:S(2)}, u32[]{:S(2)}) async-start(f32[4,529,192]{1,2,0:T(8,128)} %copy.75), calls=%async_computation.1 | async-start | bytes 3932160 | tf_op jit(solution)/shard_map/all_to_all | solution.py:90
  1992.5 9.9 copy-start.13
  1992.5 256.8 %reduce-scatter.25.cloned.1.call-start = ((), (), s32[]{:S(2)}) async-start(), calls=%async_computation.15 | async-start | bytes 884736
  2006.6 8.1 copy-start.26
  2092.4 191.9 %reduce-scatter.23.cloned.1.call-start = ((), (), s32[]{:S(2)}) async-start(), calls=%async_computation.14 | async-start | bytes 2211840
  2176.4 8.2 collective-permute-start.3
  (17 other events, 92.5 us)
Sparse Core Ops, SparseCore 0:
  12.3 32.0 all-gather.12
  47.5 28.7 all-gather.18
  230.8 34.1 all-gather.14
  1198.1 222.6 all-gather.20
  1422.2 223.6 all-gather.16
  1671.5 228.7 all-reduce.13
  1924.2 13.7 reduce-scatter.26
  1940.9 13.1 reduce-scatter.28
  1969.8 28.1 all-gather.22
  2092.6 62.4 reduce-scatter.24
  2158.9 65.6 reduce-scatter.22
where the time goes:
time: 2340 us; the launch traced here: 2330 us
  blocking collectives  1120 us (48%)
  waiting for transfers between devices  702 us (30%)
  local copies, waits for them, and re-layouts  231 us (10%)
  matrix products  151 us (6%)
  other arithmetic  75.5 us (3%)
  starting transfers between devices  28 us (1%)
    unnamed x4, blocking collectives  994 us
    all_gather x2, waiting for transfers between devices, gather_columns(): return lax.all_gather(local_rows, 'mod', axis=0, tiled=True)  420 us
    unnamed x20, waiting for transfers between devices  229 us
    unnamed x92, local copies, waits for them, and re-layouts  146 us
  transfers between devices with their start and end apart: 19, of which 6 were waited for; matrix products, arithmetic and copies ran while one was open for 58% of the time, Pallas kernels for 0%

commit v1 on v0

v1 whole, which is shorter than its diff:
```python
import functools

import jax
import jax.numpy as jnp
from jax import lax
from jax.experimental import pallas as pl
from jax.experimental.pallas import tpu as pltpu
from jax.sharding import PartitionSpec as P

HEAD = 64
U = 529
ROWS = 544
EPSILON = 1e-06
MASKED = -1000000000.0
SCALE = HEAD**-0.5
F32 = jnp.float32
BF16 = jnp.bfloat16
VMEM = pl.BlockSpec(memory_space=pltpu.VMEM)
SMEM = pl.BlockSpec(memory_space=pltpu.SMEM)


def dot(a, b, ca=1, cb=0):
    return lax.dot_general(a, b, (((ca,), (cb,)), ((), ())), preferred_element_type=F32)


def call(kernel, outs, specs, name, flops, aliases=None):
    nbytes = sum(o.size * o.dtype.itemsize for o in outs)
    return pl.pallas_call(
        kernel,
        out_shape=outs,
        in_specs=specs,
        out_specs=[VMEM] * len(outs),
        input_output_aliases=aliases or {},
        compiler_params=pltpu.CompilerParams(vmem_limit_bytes=50 * 1024 * 1024),
        cost_estimate=pl.CostEstimate(
            flops=int(flops), bytes_accessed=int(3 * nbytes), transcendentals=0
        ),
        name=name,
    )


def shape(*dims, dtype=F32):
    return jax.ShapeDtypeStruct(dims, dtype)


def normed(x):
    mean = jnp.mean(x, axis=1, keepdims=True)
    spread = jnp.mean(x * x, axis=1, keepdims=True) - mean * mean
    inverse = lax.rsqrt(spread + EPSILON)
    return (x - mean) * inverse, inverse


def norm_back(upstream, xhat, inverse, gain):
    scaled = upstream * gain
    first = jnp.mean(scaled, axis=1, keepdims=True)
    second = jnp.mean(scaled * xhat, axis=1, keepdims=True)
    return inverse * (scaled - first - xhat * second)


def ln1_kernel(x_ref, g_ref, b_ref, n_ref):
    xhat, _ = normed(x_ref[...].astype(F32))
    n_ref[...] = (xhat * g_ref[...] + b_ref[...]).astype(BF16)


def allowed_mask(meta_ref):
    kind, first, second, offset = meta_ref[0], meta_ref[1], meta_ref[2], meta_ref[3]
    start = jnp.where(kind == 1, offset, U)
    key = lax.broadcasted_iota(jnp.int32, (ROWS, 1), 0)
    query = lax.broadcasted_iota(jnp.int32, (1, ROWS), 1)
    key_upper = key >= start
    limit = jnp.where(key < U, jnp.where(key_upper, second, first), 0)
    place = jnp.where(key_upper, key - start, key)
    key_code = jnp.where(place < limit, jnp.where(key_upper, 1, 0), 2)
    query_code = jnp.where(query >= start, 1, 0)
    return key_code == query_code


def attn_fwd_kernel(meta_ref, n1_ref, w_ref, proj_ref, ho_ref, lse_ref):
    width = w_ref.shape[0] // 3
    proj = dot(w_ref[...], n1_ref[...], 1, 1)
    proj_ref[0:width, :] = (proj[0:width] * SCALE).astype(BF16)
    proj_ref[width:, :] = proj[width:].astype(BF16)
    allowed = allowed_mask(meta_ref)
    lse_ref[...] = jnp.zeros_like(lse_ref)
    for h in range(width // HEAD):
        q = proj_ref[h * HEAD : (h + 1) * HEAD, :]
        k = proj_ref[width + h * HEAD : width + (h + 1) * HEAD, :]
        v = proj_ref[2 * width + h * HEAD : 2 * width + (h + 1) * HEAD, :]
        s = jnp.where(allowed, dot(k, q, 0, 0), MASKED)
        m = jnp.max(s, axis=0, keepdims=True)
        e = jnp.exp(s - m)
        total = jnp.sum(e, axis=0, keepdims=True)
        p = (e * (1.0 / total)).astype(BF16)
        ho_ref[h * HEAD : (h + 1) * HEAD, :] = dot(v, p, 1, 0).astype(BF16)
        lse_ref[h : h + 1, :] = m + jnp.log(total)


def mid_kernel(tok_ref, cot_ref, g_ref, b_ref, *refs):
    blocks = (len(refs) - 4) // 2
    mid_ref, n2_ref, n2t_ref, cott_ref = refs[2 * blocks :]
    acc = tok_ref[...].astype(F32)
    for j in range(blocks):
        acc += dot(refs[j][...], refs[blocks + j][...], 0, 0)
    mid_ref[...] = acc
    xhat, _ = normed(acc)
    n2 = (xhat * g_ref[...] + b_ref[...]).astype(BF16)
    n2_ref[...] = n2
    n2t_ref[...] = n2.T
    cott_ref[...] = cot_ref[...].T


def ffn_kernel(first, n2_ref, n2t_ref, cot_ref, cott_ref, up_ref, down_ref, *refs):
    if first:
        branch_ref, dn2_ref, grad_ref = refs
    else:
        branch_in, dn2_in, branch_ref, dn2_ref, grad_ref = refs
    d = up_ref.shape[0]
    tile = 256
    for t in range(d // tile):
        cols = slice(t * tile, (t + 1) * tile)
        hidden = dot(n2_ref[...], up_ref[:, cols])
        d_act = dot(cot_ref[...], down_ref[:, cols])
        cdf = 0.5 * (1.0 + lax.erf(hidden * (0.5**0.5)))
        pdf = jnp.exp(-0.5 * hidden * hidden) * 0.3989422804014327
        act = (hidden * cdf).astype(BF16)
        d_hid = (d_act * (cdf + hidden * pdf)).astype(BF16)
        b_part = dot(act, down_ref[:, cols], 1, 1)
        d_part = dot(d_hid, up_ref[:, cols], 1, 1)
        if t == 0:
            if first:
                branch_ref[...] = b_part
                dn2_ref[...] = d_part
            else:
                branch_ref[...] = branch_in[...] + b_part
                dn2_ref[...] = dn2_in[...] + d_part
        else:
            branch_ref[...] += b_part
            dn2_ref[...] += d_part
        grad_ref[0:d, cols] = dot(n2t_ref[...], d_hid).astype(BF16)
        grad_ref[d : 2 * d, cols] = dot(cott_ref[...], act).astype(BF16)


def mid2_kernel(mid_ref, branch_ref, dn2_ref, cot_ref, g_ref, out_ref, dmid_ref, datt_ref, gg_ref, bg_ref):
    mid = mid_ref[...]
    out_ref[...] = (mid + branch_ref[...])[:U].astype(BF16)
    xhat, inverse = normed(mid)
    up = dn2_ref[...]
    dmid = cot_ref[...].astype(F32) + norm_back(up, xhat, inverse, g_ref[...])
    dmid_ref[...] = dmid
    datt_ref[...] = dmid.astype(BF16)
    gg_ref[...] = jnp.sum(up * xhat, axis=0, keepdims=True)
    bg_ref[...] = jnp.sum(up, axis=0, keepdims=True)


def attn_bwd_kernel(first, meta_ref, proj_ref, lse_ref, ho_ref, datt_ref, n1_ref, w_ref, wo_ref, *refs):
    if first:
        dn1_ref, grad_ref, dproj_ref = refs
    else:
        dn1_in, dn1_ref, grad_ref, dproj_ref = refs
    width = wo_ref.shape[0]
    allowed = allowed_mask(meta_ref)
    datt = datt_ref[...]
    dheads = dot(wo_ref[...], datt, 1, 1).astype(BF16)
    grad_ref[3 * width :, :] = dot(ho_ref[...], datt).astype(BF16)
    for h in range(width // HEAD):
        rows = slice(h * HEAD, (h + 1) * HEAD)
        q = proj_ref[h * HEAD : (h + 1) * HEAD, :]
        k = proj_ref[width + h * HEAD : width + (h + 1) * HEAD, :]
        v = proj_ref[2 * width + h * HEAD : 2 * width + (h + 1) * HEAD, :]
        do = dheads[rows]
        s = jnp.where(allowed, dot(k, q, 0, 0), MASKED)
        p = jnp.exp(s - lse_ref[h : h + 1, :])
        dp = dot(v, do, 0, 0)
        delta = jnp.sum(p * dp, axis=0, keepdims=True)
        ds = (p * (dp - delta)).astype(BF16)
        dproj_ref[h * HEAD : (h + 1) * HEAD, :] = (dot(k, ds, 1, 0) * SCALE).astype(BF16)
        dproj_ref[width + h * HEAD : width + (h + 1) * HEAD, :] = dot(q, ds, 1, 1).astype(BF16)
        dproj_ref[2 * width + h * HEAD : 2 * width + (h + 1) * HEAD, :] = dot(
            do, p.astype(BF16), 1, 1
        ).astype(BF16)
    dproj = dproj_ref[...]
    grad_ref[0 : 3 * width, :] = dot(dproj, n1_ref[...]).astype(BF16)
    part = dot(dproj, w_ref[...], 0, 0)
    if first:
        dn1_ref[...] = part
    else:
        dn1_ref[...] = dn1_in[...] + part


def final_kernel(tok_ref, dmid_ref, dn1_ref, g_ref, out_ref, gg_ref, bg_ref):
    xhat, inverse = normed(tok_ref[...].astype(F32))
    up = dn1_ref[...]
    out_ref[...] = (dmid_ref[...] + norm_back(up, xhat, inverse, g_ref[...]))[:U].astype(BF16)
    gg_ref[...] = jnp.sum(up * xhat, axis=0, keepdims=True)
    bg_ref[...] = jnp.sum(up, axis=0, keepdims=True)


def body(
    tokens,
    cotangent,
    unit_kind,
    unit_len,
    pack_offset,
    norm1_gain,
    norm1_bias,
    qkv_weight,
    out_weight,
    norm2_gain,
    norm2_bias,
    up_weight,
    down_weight,
):
    hid = lax.axis_size("hid")
    mod = lax.axis_size("mod")
    d = tokens.shape[1]
    width = out_weight.shape[0]
    unit = (lax.axis_index("dp") * hid + lax.axis_index("hid")) * mod + lax.axis_index("mod")
    meta = jnp.stack(
        [unit_kind[unit], unit_len[unit, 0], unit_len[unit, 1], pack_offset[unit]]
    )
    tok = jnp.pad(tokens, ((0, ROWS - U), (0, 0)))
    cot = jnp.pad(cotangent, ((0, ROWS - U), (0, 0)))
    g1, b1, g2, b2 = (v[None] for v in (norm1_gain, norm1_bias, norm2_gain, norm2_bias))

    qo = jnp.concatenate([qkv_weight.reshape(3 * width, d), out_weight], axis=0)
    qo = lax.all_gather(qo, "hid")
    ff = lax.all_gather(jnp.stack([up_weight, down_weight]), ("hid", "mod"))
    ff = ff.reshape(hid, mod, 2, d // mod, d)
    w = [qo[j, : 3 * width] for j in range(hid)]
    wo = [qo[j, 3 * width :] for j in range(hid)]
    up = [ff[j, :, 0].reshape(d, d) for j in range(hid)]
    down = [ff[j, :, 1].reshape(d, d) for j in range(hid)]

    row = shape(ROWS, d)
    row16 = shape(ROWS, d, dtype=BF16)
    wide16 = shape(d, ROWS, dtype=BF16)
    vec = shape(1, d)
    mm = 2 * ROWS * d * d
    (n1,) = call(ln1_kernel, [row16], [VMEM] * 3, "ln1", 1e7)(tok, g1, b1)
    proj, ho, lse = [], [], []
    for j in range(hid):
        a, b, c = call(
            attn_fwd_kernel,
            [shape(3 * width, ROWS, dtype=BF16), shape(width, ROWS, dtype=BF16), shape(8, ROWS)],
            [SMEM] + [VMEM] * 2,
            "attn_fwd",
            mm,
        )(meta, n1, w[j])
        proj.append(a)
        ho.append(b)
        lse.append(c)
    mid, n2, n2t, cott = call(
        mid_kernel, [row, row16, wide16, wide16], [VMEM] * (4 + 2 * hid), "mid", mm
    )(tok, cot, g2, b2, *ho, *wo)
    state = []
    ffgrads = []
    for j in range(hid):
        branch, dn2, grad = call(
            functools.partial(ffn_kernel, j == 0),
            [row, row, shape(2 * d, d, dtype=BF16)],
            [VMEM] * (6 + len(state)),
            "ffn",
            6 * mm,
            {6: 0, 7: 1} if j else None,
        )(n2, n2t, cot, cott, up[j], down[j], *state)
        state = [branch, dn2]
        ffgrads.append(grad)
    output, dmid, datt, g2g, b2g = call(
        mid2_kernel,
        [shape(U, d, dtype=BF16), row, row16, vec, vec],
        [VMEM] * 5,
        "mid2",
        1e7,
    )(mid, branch, dn2, cot, g2)
    state = []
    qograds = []
    for j in range(hid):
        dn1, grad, _ = call(
            functools.partial(attn_bwd_kernel, j == 0),
            [row, shape(d, d, dtype=BF16), shape(3 * width, ROWS, dtype=BF16)],
            [SMEM] + [VMEM] * (7 + len(state)),
            "attn_bwd",
            3 * mm,
            {8: 0} if j else None,
        )(meta, proj[j], lse[j], ho[j], datt, n1, w[j], wo[j], *state)
        state = [dn1]
        qograds.append(grad)
    tokens_grad, g1g, b1g = call(
        final_kernel, [shape(U, d, dtype=BF16), vec, vec], [VMEM] * 4, "final", 1e7
    )(tok, dmid, dn1, g1)

    ffg = jnp.stack(ffgrads).reshape(hid, 2, mod, d // mod, d).transpose(0, 2, 1, 3, 4)
    ffg = lax.psum_scatter(
        ffg.reshape(hid * mod, 2, d // mod, d), ("hid", "mod"), scatter_dimension=0, tiled=True
    )
    ffg = lax.psum(ffg, "dp")[0].astype(F32)
    qog = lax.psum_scatter(jnp.stack(qograds), "hid", scatter_dimension=0, tiled=True)
    qog = lax.psum(qog, ("dp", "mod"))[0].astype(F32)
    vecs = lax.psum(jnp.concatenate([g1g, b1g, g2g, b2g]), ("dp", "hid", "mod"))
    return (
        output,
        tokens_grad,
        vecs[0],
        vecs[1],
        qog[: 3 * width].reshape(3, width, d),
        qog[3 * width :],
        vecs[2],
        vecs[3],
        ffg[0],
        ffg[1],
    )


def solution(mesh):
    rows = P(("dp", "hid", "mod"), None)
    in_specs = (
        rows,
        rows,
        P(),
        P(),
        P(),
        P(),
        P(),
        P(None, "hid", None),
        P("hid", None),
        P(),
        P(),
        P("mod", "hid"),
        P("mod", "hid"),
    )
    out_specs = (
        rows,
        rows,
        P(),
        P(),
        P(None, "hid", None),
        P("hid", None),
        P(),
        P(),
        P("mod", "hid"),
        P("mod", "hid"),
    )
    return jax.shard_map(body, mesh=mesh, in_specs=in_specs, out_specs=out_specs, check_vma=False)
```

time: 2340 us -> 518 us (0.22)
  blocking collectives: 1120 us -> 40.8 us
  waiting for transfers between devices: 702 us -> 298 us
  local copies, waits for them, and re-layouts: 231 us -> 34.9 us
  matrix products: 151 us -> 0 us
  Pallas kernels: 0 us -> 99.5 us
  other arithmetic: 75.5 us -> 20.8 us
  starting transfers between devices: 28 us -> 0.24 us
    unnamed x4 -> x0, blocking collectives: 994 us -> none
    all_gather x6 -> x2, waiting for transfers between devices: 425 us -> 87.6 us  [the longest x1 54.1 us: body(): ff = lax.all_gather(jnp.stack([up_weight, down_weight]), ('hid', 'mod'))]
    unnamed x20 -> x6, waiting for transfers between devices: 229 us -> 0.1 us
    dot_general x39 -> x0, matrix products: 148 us -> none  [the longest x3 33.2 us: matmul_rows(): return jnp.dot(source, weight, preferred_element_type=jnp.float32)]
    reduce_scatter x0 -> x2, waiting for transfers between devices: none -> 143 us  [the longest x1 116 us: body(): lax.psum_scatter(ffg.reshape(hid * mod, 2, d // mod, d), ('hid', 'mod'),...]
    unnamed x92 -> x88, local copies, waits for them, and re-layouts: 146 us -> 7.13 us
    pallas_call x0 -> x16, Pallas kernels: none -> 99.5 us  [the longest x4 37.1 us: body(): call(functools.partial(ffn_kernel, j == 0), [row, row, shape(2 * d, d, dt...]
    all_gather x4 -> x0, blocking collectives: 82.7 us -> none  [the longest x1 38.1 us: body(): lax.all_gather(joint_share.astype(jnp.bfloat16), ('dp', 'mod'), axis=2, t...]
  transfers between devices with their start and end apart: 19 -> 6, of which waited for: 6 -> 6; matrix products, arithmetic and copies ran while one was open for 58% -> 7% of each run, Pallas kernels for 0% -> 5%
where the time goes in v1:
time: 518 us; the launch traced here: 509 us
  waiting for transfers between devices  298 us (58%)
  Pallas kernels  99.5 us (19%)
  blocking collectives  40.8 us (8%)
  local copies, waits for them, and re-layouts  34.9 us (7%)
  other arithmetic  20.8 us (4%)
  between operations  15.1 us (3%)
    reduce_scatter x1, waiting for transfers between devices, body(): lax.psum_scatter(ffg.reshape(hid * mod, 2, d // mod, d), ('hid', 'mod'),...  116 us
    all_gather x1, waiting for transfers between devices, body(): ff = lax.all_gather(jnp.stack([up_weight, down_weight]), ('hid', 'mod'))  54.1 us
    psum x1, blocking collectives, body(): vecs = lax.psum(jnp.concatenate([g1g, b1g, g2g, b2g]), ('dp', 'hid', 'mod'))  40.8 us
    psum x1, waiting for transfers between devices, body(): qog = lax.psum(qog, ('dp', 'mod'))[0].astype(F32)  38.6 us
    pallas_call x4, Pallas kernels, body(): call(functools.partial(ffn_kernel, j == 0), [row, row, shape(2 * d, d, dt...  37.1 us
    pallas_call x4, Pallas kernels, body(): call(functools.partial(attn_bwd_kernel, j == 0), [row, shape(d, d, dtype=...  34.6 us
    all_gather x1, waiting for transfers between devices, body(): qo = lax.all_gather(qo, 'hid')  33.5 us
    psum x1, waiting for transfers between devices, body(): ffg = lax.psum(ffg, 'dp')[0].astype(F32)  28.1 us
  transfers between devices with their start and end apart: 6, of which 6 were waited for; matrix products, arithmetic and copies ran while one was open for 7% of the time, Pallas kernels for 5%

profile of v1, /device:TPU:0, one launch (start us, length us, event | category | flops | bytes accessed | tf_op | source)
XLA Modules:
  0.0 508.8 jit_solution(6640097031790455745)
XLA Ops:
  7.2 2.4 pad_maximum_fusion.1
  14.2 2.7 pad_add_fusion.meta_ref
  16.9 33.5 %all-gather.5.cloned.1.call-done = bf16[3072,768]{1,0:T(8,128)(2,1)} async-done(((bf16[768,768]{1,0:T(8,128)(2,1)}), bf16[3072,768]{1,0:T(8,128)(2,1)}) %all-gather.5.cloned.1.call-update) | async-done | bytes 4718608 | tf_op jit(solution)/shard_map/all_gather | solution.py:226
  50.4 2.2 slice_bitcast_fusion
  52.6 3.8 attn_fwd.7
  58.2 3.8 attn_fwd.6
  62.0 3.8 attn_fwd.5
  66.7 3.8 attn_fwd.4
  72.5 1.7 slice_bitcast_fusion.7
  74.3 4.7 mid.1
  80.6 54.1 %all-gather.7.cloned.1.call-done = bf16[32,192,768]{2,1,0:T(8,128)(2,1)} async-done(((bf16[2,192,768]{2,1,0:T(8,128)(2,1)}), bf16[32,192,768]{2,1,0:T(8,128)(2,1)}) %all-gather.7.cloned.1.call-update) | async-done | bytes 9437200 | tf_op jit(solution)/shard_map/all_gather | solution.py:227
  134.7 7.3 %fusion = (bf16[1,4,1,192,768]{4,3,2,1,0:T(8,128)(2,1)}, bf16[1,4,1,192,768]{4,3,2,1,0:T(8,128)(2,1)}, bf16[1,4,1,192,768]{4,3,2,1,0:T(8,128)(2,1)}, bf16[1,4,1,...) fusion(bf16[4,4,2,192,768]{4,3,2,1,0:T(8,128)(2,1)} %bitcast.66), kind=kLoop, calls=%fused_computation.23 | loop fusion | bytes 18874368 | tf_op jit(solution)/shard_map/slice | solution.py:232
  142.7 8.4 %ffn.4 = (f32[544,768]{1,0:T(8,128)}, f32[544,768]{1,0:T(8,128)}, bf16[1536,768]{1,0:T(8,128)(2,1)}) custom-call(bf16[544,768]{1,0:T(8,128)(2,1)S(1)} %copy-done.20, bf16[768,544]{1,0:T(8,128)(2,1)S(1)} %copy-done.17, bf16[544,768]{1,0:T(8,128)(2,1)S(1)} %copy-done, bf16[768,544]{1,0:T(8,128)(2,1)S(1)} %copy-done.18, bf16[768,768]{1,0:T(8,128)(2,1)} %bitcast.85, ...), custom_call_target="tpu_custom_call" | custom-call | flops 3850371072 | bytes 17104896 | tf_op jit(solution)/shard_map/ffn/pallas_call | solution.py:258
  151.1 9.5 %ffn.5 = (f32[544,768]{1,0:T(8,128)}, f32[544,768]{1,0:T(8,128)}, bf16[1536,768]{1,0:T(8,128)(2,1)}) custom-call(bf16[544,768]{1,0:T(8,128)(2,1)S(1)} %copy-done.20, bf16[768,544]{1,0:T(8,128)(2,1)S(1)} %copy-done.17, bf16[544,768]{1,0:T(8,128)(2,1)S(1)} %copy-done, bf16[768,544]{1,0:T(8,128)(2,1)S(1)} %copy-done.18, ...), custom_call_target="tpu_custom_call", output_to_operand_aliasing={{0}: (6, {}), {1}: (7, {})} | custom-call | flops 3850371072 | bytes 17104896 | tf_op jit(solution)/shard_map/ffn/pallas_call | solution.py:258
  160.6 9.5 %ffn.6 = (f32[544,768]{1,0:T(8,128)}, f32[544,768]{1,0:T(8,128)}, bf16[1536,768]{1,0:T(8,128)(2,1)}) custom-call(bf16[544,768]{1,0:T(8,128)(2,1)S(1)} %copy-done.20, bf16[768,544]{1,0:T(8,128)(2,1)S(1)} %copy-done.17, bf16[544,768]{1,0:T(8,128)(2,1)S(1)} %copy-done, bf16[768,544]{1,0:T(8,128)(2,1)S(1)} %copy-done.18, ...), custom_call_target="tpu_custom_call", output_to_operand_aliasing={{0}: (6, {}), {1}: (7, {})} | custom-call | flops 3850371072 | bytes 17104896 | tf_op jit(solution)/shard_map/ffn/pallas_call | solution.py:258
  170.1 9.7 %ffn.7 = (f32[544,768]{1,0:T(8,128)}, f32[544,768]{1,0:T(8,128)}, bf16[1536,768]{1,0:T(8,128)(2,1)}) custom-call(bf16[544,768]{1,0:T(8,128)(2,1)S(1)} %copy-done.20, bf16[768,544]{1,0:T(8,128)(2,1)S(1)} %copy-done.17, bf16[544,768]{1,0:T(8,128)(2,1)S(1)} %copy-done, bf16[768,544]{1,0:T(8,128)(2,1)S(1)} %copy-done.18, ...), custom_call_target="tpu_custom_call", output_to_operand_aliasing={{0}: (6, {}), {1}: (7, {})} | custom-call | flops 3850371072 | bytes 17104896 | tf_op jit(solution)/shard_map/ffn/pallas_call | solution.py:258
  179.8 3.9 mid2.1
  183.8 8.2 %attn_bwd.4 = (f32[544,768]{1,0:T(8,128)}, bf16[768,768]{1,0:T(8,128)(2,1)}, bf16[576,544]{1,0:T(8,128)(2,1)}) custom-call(s32[4]{0:T(128)S(1)} %pad_add_fusion.meta_ref, bf16[576,544]{1,0:T(8,128)(2,1)S(1)} %copy-done.28, f32[8,544]{1,0:T(8,128)S(1)} %get-tuple-element.80.lse_ref, bf16[192,544]{1,0:T(8,128)(2,1)S(1)} %copy-done.16, ...), custom_call_target="tpu_custom_call" | custom-call | flops 1925185536 | bytes 10432512 | tf_op jit(solution)/shard_map/attn_bwd/pallas_call | solution.py:278
  192.0 8.9 %attn_bwd.5 = (f32[544,768]{1,0:T(8,128)}, bf16[768,768]{1,0:T(8,128)(2,1)}, bf16[576,544]{1,0:T(8,128)(2,1)}) custom-call(s32[4]{0:T(128)S(1)} %pad_add_fusion.meta_ref, bf16[576,544]{1,0:T(8,128)(2,1)S(1)} %copy-done.26, f32[8,544]{1,0:T(8,128)S(1)} %get-tuple-element.78.lse_ref, bf16[192,544]{1,0:T(8,128)(2,1)S(1)} %copy-done.14, ...), custom_call_target="tpu_custom_call", output_to_operand_aliasing={{0}: (8, {})} | custom-call | flops 1925185536 | bytes 10432512 | tf_op jit(solution)/shard_map/attn_bwd/pallas_call | solution.py:278
  200.9 8.7 %attn_bwd.6 = (f32[544,768]{1,0:T(8,128)}, bf16[768,768]{1,0:T(8,128)(2,1)}, bf16[576,544]{1,0:T(8,128)(2,1)}) custom-call(s32[4]{0:T(128)S(1)} %pad_add_fusion.meta_ref, bf16[576,544]{1,0:T(8,128)(2,1)S(1)} %copy-done.24, f32[8,544]{1,0:T(8,128)S(1)} %get-tuple-element.76.lse_ref, bf16[192,544]{1,0:T(8,128)(2,1)S(1)} %copy-done.12, ...), custom_call_target="tpu_custom_call", output_to_operand_aliasing={{0}: (8, {})} | custom-call | flops 1925185536 | bytes 10432512 | tf_op jit(solution)/shard_map/attn_bwd/pallas_call | solution.py:278
  209.6 8.8 %attn_bwd.7 = (f32[544,768]{1,0:T(8,128)}, bf16[768,768]{1,0:T(8,128)(2,1)}, bf16[576,544]{1,0:T(8,128)(2,1)}) custom-call(s32[4]{0:T(128)S(1)} %pad_add_fusion.meta_ref, bf16[576,544]{1,0:T(8,128)(2,1)S(1)} %copy-done.22, f32[8,544]{1,0:T(8,128)S(1)} %get-tuple-element.73.lse_ref, bf16[192,544]{1,0:T(8,128)(2,1)S(1)} %copy-done.10, ...), custom_call_target="tpu_custom_call", output_to_operand_aliasing={{0}: (8, {})} | custom-call | flops 1925185536 | bytes 10432512 | tf_op jit(solution)/shard_map/attn_bwd/pallas_call | solution.py:278
  218.4 3.5 pad_maximum_fusion
  222.0 10.0 %maximum_bitcast_fusion = bf16[4,4,2,192,768]{4,3,1,2,0:T(8,128)(2,1)} fusion(bf16[1,2,4,192,768]{4,3,2,1,0:T(8,128)(2,1)} %bitcast.72, bf16[1,2,4,192,768]{4,3,2,1,0:T(8,128)(2,1)} %bitcast.71, bf16[1,2,4,192,768]{4,3,2,1,0:T(8,128)(2,1)} %bitcast.70, bf16[1,2,4,192,768]{4,3,2,1,0:T(8,128)(2,1)} %bitcast.69), kind=kLoop, calls=%fused_computation | loop fusion | flops 14155776 | bytes 18874368 | tf_op jit(solution)/shard_map/transpose | solution.py:292
  232.0 8.6 %copy.49 = bf16[4,4,2,192,768]{4,3,2,1,0:T(8,128)(2,1)} copy(bf16[4,4,2,192,768]{4,3,1,2,0:T(8,128)(2,1)} %maximum_bitcast_fusion) | data formatting | bytes 18874368 | tf_op jit(solution)/shard_map/transpose | solution.py:292
  240.7 27.4 %reduce-scatter.3.cloned.1.call-done = bf16[1,768,768]{2,1,0:T(8,128)(2,1)} async-done(((bf16[4,768,768]{2,1,0:T(8,128)(2,1)}), bf16[1,768,768]{2,1,0:T(8,128)(2,1)}) %reduce-scatter.3.cloned.1.call-update) | async-done | bytes 1179664 | tf_op jit(solution)/shard_map/reduce_scatter | solution.py:297
  268.2 115.8 %reduce-scatter.5.cloned.1.call-done = bf16[1,2,192,768]{3,2,1,0:T(8,128)(2,1)} async-done(((bf16[16,2,192,768]{3,2,1,0:T(8,128)(2,1)}), bf16[1,2,192,768]{3,2,1,0:T(8,128)(2,1)}) %reduce-scatter.5.cloned.1.call-update) | async-done | bytes 589840 | tf_op jit(solution)/shard_map/reduce_scatter | solution.py:293
  384.1 3.6 final.1
  387.6 40.8 %psum.21 = f32[4,768]{1,0:T(4,128)S(1)} all-reduce(f32[4,768]{1,0:T(4,128)S(1)} %pad_maximum_fusion.3), channel_id=1, replica_groups=mesh['dp'=2,'hid'=4,'mod'=4] {'dp','hid','mod'}, use_global_device_ids=true, to_apply=%region_0.1 | all-reduce | flops 3072 | bytes 24576 | tf_op jit(solution)/shard_map/psum | solution.py:299
  429.0 38.6 %all-reduce.5.cloned.1.call-done = bf16[1,768,768]{2,1,0:T(8,128)(2,1)} async-done(((bf16[1,768,768]{2,1,0:T(8,128)(2,1)}), bf16[1,768,768]{2,1,0:T(8,128)(2,1)}) %all-reduce.5.cloned.1.call-update) | async-done | bytes 1179664 | tf_op jit(solution)/shard_map/psum | solution.py:298
  467.6 2.6 slice.121
  471.2 28.1 %all-reduce.7.cloned.1.call-done = bf16[1,2,192,768]{3,2,1,0:T(8,128)(2,1)} async-done(((bf16[1,2,192,768]{3,2,1,0:T(8,128)(2,1)}), bf16[1,2,192,768]{3,2,1,0:T(8,128)(2,1)}) %all-reduce.7.cloned.1.call-update) | async-done | bytes 589840 | tf_op jit(solution)/shard_map/psum | solution.py:296
  499.3 1.1 convert_element_type.12
  (116 shorter events, 14.4 us)
Async XLA Ops:
  7.2 43.2 %all-gather.5.cloned.1.call-start = ((), (), s32[]{:S(2)}) async-start(), calls=%async_computation.6 | async-start | bytes 5898240 | tf_op jit(solution)/shard_map/all_gather | solution.py:226
  9.7 125.0 %all-gather.7.cloned.1.call-start = ((), (), s32[]{:S(2)}) async-start(), calls=%async_computation.7 | async-start | bytes 10027008 | tf_op jit(solution)/shard_map/all_gather | solution.py:227
  9.8 3.2 copy-start.34
  10.7 257.4 %reduce-scatter.3.cloned.1.call-start = ((), (), s32[]{:S(2)}) async-start(), calls=%async_computation.2 | async-start | bytes 5898240 | tf_op jit(solution)/shard_map/reduce_scatter | solution.py:297
  14.2 52.5 %copy-start.7 = (bf16[544,768]{1,0:T(8,128)(2,1)}, bf16[544,768]{1,0:T(8,128)(2,1)S(1)}, u32[]{:S(2)}) copy-start(bf16[544,768]{1,0:T(8,128)(2,1)S(1)} %ln1.1.n1_ref) | copy-start | bytes 2506756
  52.6 9.5 %copy-start.4 = (bf16[576,768]{1,0:T(8,128)(2,1)}, bf16[576,768]{1,0:T(8,128)(2,1)S(1)}, u32[]{:S(2)}) copy-start(bf16[576,768]{1,0:T(8,128)(2,1)S(1)} %get-tuple-element.115.w_ref) | copy-start | bytes 2654212
  52.6 9.5 %copy-start.5 = (bf16[576,768]{1,0:T(8,128)(2,1)}, bf16[576,768]{1,0:T(8,128)(2,1)S(1)}, u32[]{:S(2)}) copy-start(bf16[576,768]{1,0:T(8,128)(2,1)S(1)} %get-tuple-element.116.w_ref) | copy-start | bytes 2654212
  58.2 16.1 %copy-start.9 = (bf16[192,544]{1,0:T(8,128)(2,1)}, bf16[192,544]{1,0:T(8,128)(2,1)S(1)}, u32[]{:S(2)}) copy-start(bf16[192,544]{1,0:T(8,128)(2,1)S(1)} %get-tuple-element.57.refs_3_.ho_ref) | copy-start | bytes 626692
  62.0 8.5 %copy-start.23 = (bf16[576,544]{1,0:T(8,128)(2,1)}, bf16[576,544]{1,0:T(8,128)(2,1)S(1)}, u32[]{:S(2)}) copy-start(bf16[576,544]{1,0:T(8,128)(2,1)S(1)} %get-tuple-element.75.proj_ref) | copy-start | bytes 1880068
  62.0 12.3 %copy-start.11 = (bf16[192,544]{1,0:T(8,128)(2,1)}, bf16[192,544]{1,0:T(8,128)(2,1)S(1)}, u32[]{:S(2)}) copy-start(bf16[192,544]{1,0:T(8,128)(2,1)S(1)} %get-tuple-element.56.refs_2_.ho_ref) | copy-start | bytes 626692
  66.7 7.6 %copy-start.13 = (bf16[192,544]{1,0:T(8,128)(2,1)}, bf16[192,544]{1,0:T(8,128)(2,1)S(1)}, u32[]{:S(2)}) copy-start(bf16[192,544]{1,0:T(8,128)(2,1)S(1)} %get-tuple-element.55.refs_1_.ho_ref) | copy-start | bytes 626692
  134.7 7.3 %copy-start = (bf16[544,768]{1,0:T(8,128)(2,1)S(1)}, bf16[544,768]{1,0:T(8,128)(2,1)}, u32[]{:S(2)}) copy-start(bf16[544,768]{1,0:T(8,128)(2,1)} %pad.8.cot_ref) | copy-start | bytes 2506756
  134.7 7.3 %copy-start.17 = (bf16[768,544]{1,0:T(8,128)(2,1)S(1)}, bf16[768,544]{1,0:T(8,128)(2,1)}, u32[]{:S(2)}) copy-start(bf16[768,544]{1,0:T(8,128)(2,1)} %get-tuple-element.60.n2t_ref) | copy-start | bytes 2506756
  134.7 7.3 %copy-start.18 = (bf16[768,544]{1,0:T(8,128)(2,1)S(1)}, bf16[768,544]{1,0:T(8,128)(2,1)}, u32[]{:S(2)}) copy-start(bf16[768,544]{1,0:T(8,128)(2,1)} %get-tuple-element.61.cott_ref) | copy-start | bytes 2506756
  134.7 8.0 %copy-start.20 = (bf16[544,768]{1,0:T(8,128)(2,1)S(1)}, bf16[544,768]{1,0:T(8,128)(2,1)}, u32[]{:S(2)}) copy-start(bf16[544,768]{1,0:T(8,128)(2,1)} %copy-done.19) | copy-start | bytes 2506756
  179.8 3.9 copy-start.2
  179.8 3.9 copy-start.8
  179.8 3.9 copy-start.16
  179.8 3.9 copy-start.28
  183.7 8.2 %copy-start.14 = (bf16[192,544]{1,0:T(8,128)(2,1)S(1)}, bf16[192,544]{1,0:T(8,128)(2,1)}, u32[]{:S(2)}) copy-start(bf16[192,544]{1,0:T(8,128)(2,1)} %copy-done.13) | copy-start | bytes 626692
  183.8 8.2 %copy-start.26 = (bf16[576,544]{1,0:T(8,128)(2,1)S(1)}, bf16[576,544]{1,0:T(8,128)(2,1)}, u32[]{:S(2)}) copy-start(bf16[576,544]{1,0:T(8,128)(2,1)} %copy-done.25) | copy-start | bytes 1880068
  191.9 8.9 %copy-start.12 = (bf16[192,544]{1,0:T(8,128)(2,1)S(1)}, bf16[192,544]{1,0:T(8,128)(2,1)}, u32[]{:S(2)}) copy-start(bf16[192,544]{1,0:T(8,128)(2,1)} %copy-done.11) | copy-start | bytes 626692
  191.9 8.9 %copy-start.24 = (bf16[576,544]{1,0:T(8,128)(2,1)S(1)}, bf16[576,544]{1,0:T(8,128)(2,1)}, u32[]{:S(2)}) copy-start(bf16[576,544]{1,0:T(8,128)(2,1)} %copy-done.23) | copy-start | bytes 1880068
  200.9 8.7 %copy-start.10 = (bf16[192,544]{1,0:T(8,128)(2,1)S(1)}, bf16[192,544]{1,0:T(8,128)(2,1)}, u32[]{:S(2)}) copy-start(bf16[192,544]{1,0:T(8,128)(2,1)} %copy-done.9) | copy-start | bytes 626692
  200.9 8.7 %copy-start.22 = (bf16[576,544]{1,0:T(8,128)(2,1)S(1)}, bf16[576,544]{1,0:T(8,128)(2,1)}, u32[]{:S(2)}) copy-start(bf16[576,544]{1,0:T(8,128)(2,1)} %copy-done.21) | copy-start | bytes 1880068
  209.6 8.8 %copy-start.30 = (bf16[768,768]{1,0:T(8,128)(2,1)S(1)}, bf16[768,768]{1,0:T(8,128)(2,1)}, u32[]{:S(2)}) copy-start(bf16[768,768]{1,0:T(8,128)(2,1)} %get-tuple-element.90) | copy-start | bytes 3538948
  209.6 8.8 %copy-start.31 = (bf16[768,768]{1,0:T(8,128)(2,1)S(1)}, bf16[768,768]{1,0:T(8,128)(2,1)}, u32[]{:S(2)}) copy-start(bf16[768,768]{1,0:T(8,128)(2,1)} %get-tuple-element.91) | copy-start | bytes 3538948
  209.6 8.8 %copy-start.32 = (bf16[768,768]{1,0:T(8,128)(2,1)S(1)}, bf16[768,768]{1,0:T(8,128)(2,1)}, u32[]{:S(2)}) copy-start(bf16[768,768]{1,0:T(8,128)(2,1)} %get-tuple-element.92) | copy-start | bytes 3538948
  222.0 162.0 %reduce-scatter.5.cloned.1.call-start = ((), (), s32[]{:S(2)}) async-start(), calls=%async_computation.4 | async-start | bytes 10027008 | tf_op jit(solution)/shard_map/reduce_scatter | solution.py:293
  240.6 227.0 %all-reduce.5.cloned.1.call-start = ((), (), s32[]{:S(2)}) async-start(), calls=%async_computation.3 | async-start | bytes 2359296 | tf_op jit(solution)/shard_map/psum | solution.py:298
  268.2 231.1 %all-reduce.7.cloned.1.call-start = ((), (), s32[]{:S(2)}) async-start(), calls=%async_computation.5 | async-start | bytes 1179648 | tf_op jit(solution)/shard_map/psum | solution.py:296
  467.6 2.6 copy-start.29
  (18 other events, 28.6 us)
Sparse Core Ops, SparseCore 0:
  10.1 40.1 all-gather.4
  53.2 81.4 all-gather.6
  222.1 45.9 reduce-scatter.2
  272.6 111.3 reduce-scatter.4
  387.4 80.1 all-reduce.4
  469.9 29.3 all-reduce.6
